TPU v7x, 256 devices: a whole 4x4x8 slice. The times are simulated.
256 devices in a mesh: var: 64 (over y, z_lo, x), samp: 4 (over z_hi, core).
Axes of the slice: x: 4, y: 4, z: 8 (z_hi: 2, z_lo: 4; z = z_hi * 4 + z_lo), core: 2. Of those that a mesh axis runs over, the one named last changes fastest.
Arguments:
- dosages: bfloat16 [16384, 32768], P('samp', 'var'), as said below
- window_end: int32 [32768], P('var'), may hold values from 0 to 32767, as said below
Outputs:
- correlations: bfloat16 [32768, 2048], P('var')
Inputs may be any that keep to these rules, and one draw needn't show every extreme that they name: For a variant in block b (of 512 variants), window_end lies in block b + 1, b + 2 or b + 3 (the same block reach for the whole block), clipped to 32767; some variant reaches the last variant of the block three ahead. `dosages`: dosages lie between 0 and 2.
All inputs are finite; a program needn't handle non-finite values.
Results may differ from a plain program's by a relative error of at most 0.0034.
Values may be sent and summed in bfloat16 or wider, within the bound.
No kernel may reach another device: no remote copies, remote signals or barrier semaphores. Data moves between devices by JAX's collectives and lax.ppermute only.
A program may use at most 64 MiB of HBM per device.

v0:
```python
import jax
import jax.numpy as jnp
from jax import lax
from jax.sharding import PartitionSpec as P


def passed_along(value, axis, steps):
    count = lax.axis_size(axis)
    first, last = (max(0, -steps), min(count, count - steps))
    return lax.ppermute(value, axis, [(source, source + steps) for source in range(first, last)])


def per_device(dosages, window_end):
    local_rows = dosages.shape[0]
    width = dosages.shape[1]
    groups = lax.axis_size("samp")
    total = local_rows * groups
    data = dosages.astype(jnp.float32)
    sums, squares = lax.psum((jnp.sum(data, axis=0), jnp.sum(data * data, axis=0)), "samp")
    mean = sums / total
    spread = 1.0 / jnp.sqrt(squares / total - mean * mean + 1e-05)
    standard = ((data - mean[None, :]) * spread[None, :]).astype(jnp.bfloat16)
    pieces = [standard]
    for step in range(1, 4):
        pieces.append(passed_along(standard, "var", -step))
    band = jnp.concatenate(pieces, axis=1)
    block_start = lax.axis_index("var") * width
    columns = jnp.arange(4 * width, dtype=jnp.int32)
    gram = lax.psum(
        jnp.einsum("sa,sb->ab", standard, band, preferred_element_type=jnp.float32), "samp"
    )
    target = block_start + columns
    keep = (columns[None, :] < width) | (target[None, :] <= window_end[:, None])
    return jnp.where(keep, gram / total, 0.0).astype(jnp.bfloat16)


def solution(mesh):
    placed = (P("samp", "var"), P("var"))
    return jax.shard_map(
        per_device, mesh=mesh, in_specs=placed, out_specs=P("var", None), check_vma=False
    )
```

profile of v0, /device:TPU:31, one launch (start us, length us, event | category | flops | bytes accessed | tf_op | source)
XLA Modules:
  0.0 743.2 jit_solution(16544478566223653503)
XLA Ops:
  6.5 0.0 all-reduce.3.cloned.1.call-start
  6.5 3.3 convert_reduce_fusion
  9.9 11.2 %all-reduce = (f32[512]{0:T(512)S(1)}, f32[512]{0:T(512)S(1)}) all-reduce(f32[512]{0:T(512)S(1)} %get-tuple-element.6, f32[512]{0:T(512)S(1)} %get-tuple-element.5), channel_id=1, replica_groups=mesh['var'=64,'samp'=4] {'samp'}, use_global_device_ids=true, to_apply=%region_3.0 | all-reduce | flops 1024 | bytes 8192 | tf_op jit(solution)/shard_map/psum | solution.py:19
  21.1 3.2 fusion.9
  24.4 2.5 collective-permute-start
  26.8 2.7 collective-permute-start.1
  29.6 6.5 collective-permute-start.2
  36.1 169.6 %collective-permute-done = bf16[4096,512]{1,0:T(8,128)(2,1)S(1)} collective-permute-done((bf16[4096,512]{1,0:T(8,128)(2,1)S(1)}, bf16[4096,512]{1,0:T(8,128)(2,1)S(1)}, u32[]{:S(2)}, u32[]{:S(2)}) %collective-permute-start) | collective-permute-done | bytes 4194336 | tf_op jit(solution)/shard_map/ppermute | solution.py:10
  205.7 0.0 collective-permute-done.1
  205.7 0.0 collective-permute-done.2
  205.7 10.9 %fusion = f32[512,2048]{1,0:T(8,128)} fusion(bf16[4096,512]{1,0:T(8,128)(2,1)S(1)} %fusion.9, bf16[4096,512]{1,0:T(8,128)(2,1)S(1)} %collective-permute-done.2, bf16[4096,512]{1,0:T(8,128)(2,1)S(1)} %collective-permute-done.1, bf16[4096,512]{1,0:T(8,128)(2,1)S(1)} %collective-permute-done), kind=kOutput, calls=%fused_computation | convolution fusion | flops 8657043456 | bytes 20971520 | tf_op jit(solution)/shard_map/sa,sb->ab/dot_general | solution.py:30
  216.6 0.0 copy-start
  216.6 0.0 all-reduce.3.cloned.1.call-update
  216.6 515.2 %all-reduce.3.cloned.1.call-done = f32[512,2048]{1,0:T(8,128)} async-done(((f32[512,2048]{1,0:T(8,128)}), f32[512,2048]{1,0:T(8,128)}) %all-reduce.3.cloned.1.call-update) | async-done | bytes 4194320 | tf_op jit(solution)/shard_map/psum | solution.py:29
  731.8 0.0 copy-done
  731.8 4.5 select_convert_fusion
  (3 shorter events, 0.0 us)
Async XLA Ops:
  6.5 725.3 %all-reduce.3.cloned.1.call-start = ((), (), s32[]{:S(2)}) async-start(), calls=%async_computation | async-start | bytes 8388608 | tf_op jit(solution)/shard_map/psum | solution.py:29
  24.4 181.3 %collective-permute-start = (bf16[4096,512]{1,0:T(8,128)(2,1)S(1)}, bf16[4096,512]{1,0:T(8,128)(2,1)S(1)}, u32[]{:S(2)}, u32[]{:S(2)}) collective-permute-start(bf16[4096,512]{1,0:T(8,128)(2,1)S(1)} %fusion.9), channel_id=1, source_target_pairs={{4,0},{8,4},{12,8},{16,12},{20,16},{24,20},{28,24},{32,28},{36,32}... | collective-permute-start | bytes 12582920 | tf_op jit(solution)/shard_map/ppermute | solution.py:10
  26.8 178.8 %collective-permute-start.1 = (bf16[4096,512]{1,0:T(8,128)(2,1)S(1)}, bf16[4096,512]{1,0:T(8,128)(2,1)S(1)}, u32[]{:S(2)}, u32[]{:S(2)}) collective-permute-start(bf16[4096,512]{1,0:T(8,128)(2,1)S(1)} %fusion.9), channel_id=1, source_target_pairs={{8,0},{12,4},{16,8},{20,12},{24,16},{28,20},{32,24},{36,28},{40,32... | collective-permute-start | bytes 12582920 | tf_op jit(solution)/shard_map/ppermute | solution.py:10
  29.6 176.1 %collective-permute-start.2 = (bf16[4096,512]{1,0:T(8,128)(2,1)S(1)}, bf16[4096,512]{1,0:T(8,128)(2,1)S(1)}, u32[]{:S(2)}, u32[]{:S(2)}) collective-permute-start(bf16[4096,512]{1,0:T(8,128)(2,1)S(1)} %fusion.9), channel_id=1, source_target_pairs={{12,0},{16,4},{20,8},{24,12},{28,16},{32,20},{36,24},{40,28},{44,3... | collective-permute-start | bytes 12582920 | tf_op jit(solution)/shard_map/ppermute | solution.py:10
  216.6 515.2 %copy-start = (s32[512]{0:T(512)S(1)}, s32[512]{0:T(512)}, u32[]{:S(2)}) copy-start(s32[512]{0:T(512)} %param.3) | copy-start | bytes 6148
Sparse Core Ops, SparseCore 0:
  216.7 515.0 all-reduce.2
where the time goes:
time: 745 us; the launch traced here: 743 us
  waiting for transfers between devices  685 us (92%)
  between operations  13.4 us (2%)
  starting transfers between devices  11.7 us (2%)
  blocking collectives  11.2 us (2%)
  other arithmetic  11.1 us (1%)
  matrix products  10.9 us (1%)
    psum x1, waiting for transfers between devices, per_device(): lax.psum(jnp.einsum('sa,sb->ab', standard, band, preferred_element_type=j...  515 us
    ppermute x3, waiting for transfers between devices, passed_along(): lax.ppermute(value, axis, [(source, source + steps) for source in range(f...  170 us
  transfers between devices with their start and end apart: 4, of which 2 were waited for; matrix products, arithmetic and copies ran while one was open for 0% of the time, Pallas kernels for 0%

commit v1 on v0

v1 whole, which is shorter than its diff:
```python
import jax
import jax.numpy as jnp
from jax import lax
from jax.experimental import pallas as pl
from jax.experimental.pallas import tpu as pltpu
from jax.sharding import PartitionSpec as P

AXES = ("var", "samp")
RING = 4
GROUPS = 4
EXTRA = 16


def moved(value, pairs):
    return lax.ppermute(value, AXES, pairs)


def pairs_of(count, target):
    pairs = []
    for var in range(count):
        for samp in range(GROUPS):
            to = target(var, samp)
            if to is not None:
                pairs.append((var * GROUPS + samp, to[0] * GROUPS + to[1]))
    return pairs


def to_core(count):
    return pairs_of(count, lambda var, samp: (var, samp ^ 1))


def to_far(count):
    return pairs_of(count, lambda var, samp: (var, samp ^ 2))


def along_ring(count, step):
    return pairs_of(
        count, lambda var, samp: (var // RING * RING + (var + step) % RING, samp)
    )


def to_ring_before(count, step=None):
    def target(var, samp):
        if var < RING or (step is not None and var % RING == RING - 1):
            return None
        return (var // RING * RING - RING + (var + (step or 0)) % RING, samp)

    return pairs_of(count, target)


ANYWHERE = pl.BlockSpec(memory_space=pl.ANY)
SCALARS = pl.BlockSpec(memory_space=pltpu.SMEM)
WHOLE = pl.BlockSpec(memory_space=pltpu.VMEM)


def settings(mebibytes=56):
    return pltpu.CompilerParams(vmem_limit_bytes=mebibytes * 1024 * 1024)


FREE = pl.CostEstimate(flops=0, bytes_accessed=0, transcendentals=0)


def quarters_of(place, dosages, stats):
    rows, width = dosages.shape
    depth = rows // RING

    def kernel(place, data, stats, *refs):
        outs, every, sems = refs[:RING], refs[RING], refs[-1]
        copies = []
        for index in range(RING):
            start = pl.multiple_of(lax.rem(place[0] + index, RING) * depth, depth)
            for source, out, sem in (
                (data.at[pl.ds(start, depth), :], outs[index], 0),
                (data.at[pl.ds(index * depth, depth), :], every.at[index], 1),
            ):
                target = out.at[pl.ds(0, depth), :]
                copies.append(pltpu.make_async_copy(source, target, sems.at[sem, index]))
        for copy in copies:
            copy.start()
        terms, rest = [], stats[...]
        for _ in range(3):
            term = rest.astype(jnp.bfloat16)
            terms.append(term.astype(jnp.float32))
            rest = rest - terms[-1]
        terms.append(jnp.zeros((EXTRA - 9, width), jnp.float32))
        terms = jnp.concatenate(terms, axis=0).astype(jnp.bfloat16)
        for index in range(RING):
            outs[index][depth:, :] = terms
            every[index, depth:, :] = terms
        for copy in copies:
            copy.wait()

    return pl.pallas_call(
        kernel,
        in_specs=[SCALARS, ANYWHERE, WHOLE],
        out_specs=[WHOLE] * (RING + 1),
        out_shape=[jax.ShapeDtypeStruct((depth + EXTRA, width), dosages.dtype)] * RING
        + [jax.ShapeDtypeStruct((RING, depth + EXTRA, width), dosages.dtype)],
        scratch_shapes=[pltpu.SemaphoreType.DMA((2, RING))],
        compiler_params=settings(),
        cost_estimate=FREE,
    )(place, dosages, stats)


def carried(rows):
    rows = rows.astype(jnp.float32)
    return (rows[0:3] + rows[3:6]) + rows[6:9]


def standardized(piece, stats):
    piece = piece.astype(jnp.float32)
    return ((piece - stats[0:1, :]) * stats[1:2, :]).astype(jnp.bfloat16)


def own_product(place, dosages, stats):
    rows, width = dosages.shape
    half, chunk = width // 2, 1024

    def kernel(place, data, stats, kept, given, total, turned):
        step = pl.program_id(0)
        flat = standardized(data[...], stats)
        for start in range(0, chunk, 256):
            turned[:, start : start + 256] = flat[start : start + 256, :].T
        product = jnp.dot(turned[...], flat, preferred_element_type=jnp.float32)

        @pl.when(step == 0)
        def _():
            total[...] = product

        @pl.when(step > 0)
        def _():
            total[...] += product

        @pl.when(step == pl.num_programs(0) - 1)
        def _():
            core = place[1]
            kept[...] = total[pl.ds(pl.multiple_of(core * half, half), half), :]
            other = total[pl.ds(pl.multiple_of((1 - core) * half, half), half), :]
            given[...] = other.astype(jnp.bfloat16)

    fixed = lambda i: (0, 0)
    return pl.pallas_call(
        kernel,
        grid=(rows // chunk,),
        in_specs=[
            SCALARS,
            pl.BlockSpec((chunk, width), lambda i: (i, 0)),
            pl.BlockSpec(stats.shape, fixed),
        ],
        out_specs=[pl.BlockSpec((half, width), fixed)] * 2,
        out_shape=[
            jax.ShapeDtypeStruct((half, width), jnp.float32),
            jax.ShapeDtypeStruct((half, width), jnp.bfloat16),
        ],
        scratch_shapes=[
            pltpu.VMEM((width, width), jnp.float32),
            pltpu.VMEM((width, chunk), jnp.bfloat16),
        ],
        compiler_params=settings(),
        cost_estimate=FREE,
    )(place, dosages, stats)


def prepared(place, quarters, after):
    count, depth, width = quarters.shape
    depth -= EXTRA
    half = width // 2

    def kernel(place, raw, *refs):
        out, kept, given, stats = refs[-4:]
        stats[0] = carried(raw[0, depth:, :])
        out[0] = standardized(raw[0, :depth, :], stats.at[0])
        core = place[1]
        kept[0] = out[0, :, pl.ds(pl.multiple_of(core * half, half), half)]
        given[0] = out[0, :, pl.ds(pl.multiple_of((1 - core) * half, half), half)]

    shapes = [(2 * count, depth, width)] + [(count, depth, half)] * 2
    whole = lambda *shape: pl.BlockSpec((1, *shape), lambda i: (i, 0, 0))
    return pl.pallas_call(
        kernel,
        grid=(count,),
        in_specs=[SCALARS, whole(depth + EXTRA, width)] + [ANYWHERE] * len(after),
        out_specs=[whole(*shape[1:]) for shape in shapes] + [whole(3, width)],
        out_shape=[jax.ShapeDtypeStruct(shape, jnp.bfloat16) for shape in shapes]
        + [jax.ShapeDtypeStruct((count, 3, width), jnp.float32)],
        compiler_params=settings(),
        cost_estimate=FREE,
    )(place, quarters, *after)


def prepared_ahead(place, quarters, blocks):
    depth, width = quarters[0].shape
    depth -= EXTRA

    def kernel(place, *refs):
        raw, (out, stats, held, sems) = refs[:RING], refs[-4:]
        item = pl.program_id(0)
        for index in range(RING):
            copy = pltpu.make_async_copy(raw[index], held.at[index], sems.at[index])
            pl.when(item == 0)(copy.start)
        for index in range(RING):
            copy = pltpu.make_async_copy(raw[index], held.at[index], sems.at[index])
            pl.when(item == index)(copy.wait)
        stats[0] = carried(held[item, depth:, :])
        out[0] = standardized(held[item, :depth, :], stats.at[0])

    block = lambda i, place: lax.rem(place[0] + i, RING)
    return pl.pallas_call(
        kernel,
        grid_spec=pltpu.PrefetchScalarGridSpec(
            num_scalar_prefetch=1,
            grid=(RING,),
            in_specs=[ANYWHERE] * (RING + 1),
            out_specs=[
                pl.BlockSpec((1, depth, width), lambda i, place: (RING + block(i, place), 0, 0)),
                pl.BlockSpec((1, 3, width), lambda i, place: (block(i, place), 0, 0)),
            ],
            scratch_shapes=[
                pltpu.VMEM((RING, depth + EXTRA, width), jnp.bfloat16),
                pltpu.SemaphoreType.DMA((RING,)),
            ],
        ),
        out_shape=[
            jax.ShapeDtypeStruct(blocks.shape, blocks.dtype),
            jax.ShapeDtypeStruct((RING, 3, width), jnp.float32),
        ],
        input_output_aliases={1 + RING: 0},
        compiler_params=settings(),
        cost_estimate=FREE,
    )(place, *quarters, blocks)


def summed(own, parts, shared, after):
    half, width = own.shape
    count = len(parts)

    def kernel(own, *refs):
        parts, shared, out = refs[:count], refs[count], refs[-1]
        total = own[...]
        for part in parts:
            total = total + part[...].astype(jnp.float32)
        out[...] = (total - shared[...]).astype(jnp.bfloat16)

    return pl.pallas_call(
        kernel,
        in_specs=[WHOLE] * (count + 2) + [ANYWHERE] * len(after),
        out_shape=jax.ShapeDtypeStruct((half, width), jnp.bfloat16),
        compiler_params=settings(8),
        cost_estimate=FREE,
    )(own, *parts, shared, *after)


def assembled(place, mine, theirs):
    half, width = mine[0].shape
    count = len(mine)

    def kernel(place, *refs):
        out = refs[-1]
        core = place[1]
        for index in range(count):
            columns = slice(index * width, (index + 1) * width)
            out[pl.ds(pl.multiple_of(core * half, half), half), columns] = refs[index][...]
            out[pl.ds(pl.multiple_of((1 - core) * half, half), half), columns] = refs[
                count + index
            ][...]

    return pl.pallas_call(
        kernel,
        in_specs=[SCALARS] + [WHOLE] * (2 * count),
        out_shape=jax.ShapeDtypeStruct((2 * half, count * width), jnp.bfloat16),
        compiler_params=settings(),
        cost_estimate=FREE,
    )(place, *mine, *theirs)


def per_device(dosages, window_end):
    rows, width = dosages.shape
    count = lax.axis_size("var")
    total = rows * lax.axis_size("samp")
    var, samp = lax.axis_index("var"), lax.axis_index("samp")
    x, core = var % RING, samp % 2
    half = width // 2
    place = jnp.stack([x, core]).astype(jnp.int32)

    core_pairs, far_pairs = to_core(count), to_far(count)
    rings = [list(range(first, first + RING)) for first in range(0, count, RING)]

    data = dosages.astype(jnp.float32)
    sums = jnp.stack([jnp.sum(data, axis=0), jnp.sum(data * data, axis=0)])
    sums = jnp.stack([sums, moved(sums, far_pairs)])
    sums, far_sums = sums + moved(sums, core_pairs)
    mean = (sums[0] + far_sums[0]) / total
    spread = 1.0 / jnp.sqrt((sums[1] + far_sums[1]) / total - mean * mean + 1e-05)
    tilt = (sums[0] - far_sums[0]) / total * spread * (total / 2) ** 0.5
    own_stats = jnp.stack([mean, spread, tilt])

    *quarters, every = quarters_of(place, dosages, own_stats)
    ahead = [
        moved(quarters[-d % RING], to_ring_before(count, -d % RING)) for d in range(RING)
    ]
    here = lax.all_to_all(every, "var", 0, 0, axis_index_groups=rings)

    own_kept, own_given = own_product(place, dosages, own_stats)
    own = own_kept + moved(own_given, core_pairs).astype(jnp.float32)
    rising = lax.dynamic_slice_in_dim(tilt, core * half, half, 0)[:, None]
    values = [(own - rising * tilt[None, :]).astype(jnp.bfloat16)]
    blocks, kept_rows, given_rows, ring_stats = prepared(place, here, values)
    blocks, ahead_stats = prepared_ahead(place, ahead, blocks)
    tilts = jnp.concatenate([ring_stats[:, 2], ahead_stats[:, 2]])

    ends = lax.dynamic_slice_in_dim(window_end, core * half, half, 0)
    columns = jnp.arange(width, dtype=jnp.int32)

    def shared(step):
        return rising * lax.dynamic_slice_in_dim(tilts, x + step, 1, 0)

    def finished(step, value, other):
        both = rising * tilt[None, :] if step == 0 else shared(step)
        gram = value.astype(jnp.float32) + other.astype(jnp.float32) + 2.0 * both
        if step:
            target = (var + step) * width + columns
            gram = jnp.where(target[None, :] <= ends[:, None], gram, 0.0)
        return (gram / total).astype(jnp.bfloat16)

    far = [moved(values[0], far_pairs)]
    mine = [finished(0, values[0], far[0])]
    theirs = [moved(mine[0], core_pairs)]
    for step in (1, 2, 3):
        product = lambda left: jnp.einsum(
            "zsa,zsb->zab",
            left,
            blocks[step : step + RING],
            preferred_element_type=jnp.float32,
        )
        received = moved(product(given_rows).astype(jnp.bfloat16), core_pairs)
        kept = product(kept_rows)

        def part(d):
            at = lambda array: lax.dynamic_index_in_dim(array, (x + d) % RING, 0, False)
            return at(kept) + at(received).astype(jnp.float32)

        parts = [
            moved(part(d).astype(jnp.bfloat16), along_ring(count, d)) for d in (1, 3, 2)
        ]
        after = theirs[step - 2 : step - 1] if step > 1 else []
        values.append(summed(part(0), parts, shared(step), after))
        far.append(moved(values[step], far_pairs))
        mine.append(finished(step, values[step], far[step]))
        theirs.append(moved(mine[step], core_pairs))
    return assembled(place, mine, theirs)


def solution(mesh):
    placed = (P("samp", "var"), P("var"))
    return jax.shard_map(
        per_device, mesh=mesh, in_specs=placed, out_specs=P("var", None), check_vma=False
    )
```

time: 745 us -> 244 us (0.33)
  waiting for transfers between devices: 685 us -> 130 us
  starting transfers between devices: 11.7 us -> 62.8 us
  Pallas kernels: 0 us -> 29.4 us
  between operations: 13.4 us -> 0.41 us
  blocking collectives: 11.2 us -> 0 us
    psum x1 -> x0, waiting for transfers between devices: 515 us -> none  [per_device(): lax.psum(jnp.einsum('sa,sb->ab', standard, band, preferred_element_type=j...]
    ppermute x3 -> x27, waiting for transfers between devices: 170 us -> 50.9 us  [moved(): return lax.ppermute(value, AXES, pairs)]
    all_to_all x0 -> x1, waiting for transfers between devices: none -> 78.7 us  [per_device(): here = lax.all_to_all(every, 'var', 0, 0, axis_index_groups=rings)]
    ppermute x3 -> x27, starting transfers between devices: 11.7 us -> 57.7 us  [moved(): return lax.ppermute(value, AXES, pairs)]
    pallas_call x0 -> x8, Pallas kernels: none -> 29.4 us  [the longest x1 7.67 us: quarters_of(): pl.pallas_call(kernel, in_specs=[SCALARS, ANYWHERE, WHOLE], out_specs=[WH...]
    psum x1 -> x0, blocking collectives: 11.2 us -> none  [per_device(): lax.psum((jnp.sum(data, axis=0), jnp.sum(data * data, axis=0)), 'samp')]
  transfers between devices with their start and end apart: 4 -> 28, of which waited for: 2 -> 12; matrix products, arithmetic and copies ran while one was open for 0% -> 3% of each run, Pallas kernels for 0% -> 5%
where the time goes in v1:
time: 244 us
  waiting for transfers between devices  130 us (53%)
  starting transfers between devices  62.8 us (26%)
  Pallas kernels  29.4 us (12%)
  matrix products  10.1 us (4%)
  other arithmetic  8.39 us (3%)
  local copies, waits for them, and re-layouts  2.94 us (1%)
    all_to_all x1, waiting for transfers between devices, per_device(): here = lax.all_to_all(every, 'var', 0, 0, axis_index_groups=rings)  78.7 us
    ppermute x27, starting transfers between devices, moved(): return lax.ppermute(value, AXES, pairs)  57.7 us
    ppermute x27, waiting for transfers between devices, moved(): return lax.ppermute(value, AXES, pairs)  50.9 us
    dot_general x6, matrix products, per_device(): jnp.einsum('zsa,zsb->zab', left, blocks[step:step + RING], preferred_elem...  10.1 us
    pallas_call x1, Pallas kernels, quarters_of(): pl.pallas_call(kernel, in_specs=[SCALARS, ANYWHERE, WHOLE], out_specs=[WH...  7.67 us
    pallas_call x1, Pallas kernels, prepared(): pl.pallas_call(kernel, grid=(count,), in_specs=[SCALARS, whole(depth + EX...  6.73 us
    pallas_call x1, Pallas kernels, own_product(): pl.pallas_call(kernel, grid=(rows // chunk,), in_specs=[SCALARS, pl.Block...  6 us
    pallas_call x1, Pallas kernels, prepared_ahead(): pl.pallas_call(kernel, grid_spec=pltpu.PrefetchScalarGridSpec(num_scalar_...  5.6 us
  transfers between devices with their start and end apart: 28, of which 12 were waited for; matrix products, arithmetic and copies ran while one was open for 3% of the time, Pallas kernels for 5%

profile of v1, /device:TPU:31, one launch (start us, length us, event | category | flops | bytes accessed | tf_op | source)
XLA Modules:
  0.0 243.7 jit_solution(9564449542355851095)
XLA Ops:
  0.0 3.3 %convert_reduce_fusion = (f32[512]{0:T(512)S(1)}, f32[512]{0:T(512)S(1)}) fusion(bf16[4096,512]{1,0:T(8,128)(2,1)} %data.3), kind=kLoop, calls=%fused_computation.1 | loop fusion | flops 8387584 | bytes 4198400 | tf_op jit(solution)/shard_map/reduce_sum | solution.py:289
  3.3 7.0 %collective-permute-start = (f32[2,512]{1,0:T(2,128)S(1)}, f32[2,512]{1,0:T(2,128)S(1)}, u32[]{:S(2)}, u32[]{:S(2)}) collective-permute-start(f32[2,512]{1,0:T(2,128)S(1)} %get-tuple-element.53), channel_id=1, source_target_pairs={{0,2},{1,3},{2,0},{3,1},{4,6},{5,7},{6,4},{7,5},{8,10},{9,11},{10,... | collective-permute-start | bytes 12296 | tf_op jit(solution)/shard_map/ppermute | solution.py:15
  10.3 1.0 collective-permute-done
  11.3 1.5 collective-permute-start.1
  12.9 0.7 pad_add_fusion.place
  14.4 7.7 %shard_map.29 = (bf16[1040,512]{1,0:T(8,128)(2,1)}, bf16[1040,512]{1,0:T(8,128)(2,1)}, bf16[1040,512]{1,0:T(8,128)(2,1)}, bf16[1040,512]{1,0:T(8,128)(2,1)}, bf16[4,1040,512]{2,1,0:T(8,128)(2,1)}) custom-call(s32[2]{0:T(128)} %pad_add_fusion.place, bf16[4096,512]{1,0:T(8,128)(2,1)} %data.3, f32[3,512]{1,0:T(4,128)} %pad_maximum_fusion.1.stats), custom_call_target="tpu_custom_call" | custom-call | tf_op jit(solution)/shard_map/pallas_call | solution.py:93
  22.1 5.1 %all-to-all-start = ((bf16[4,1040,512]{2,1,0:T(8,128)(2,1)}), bf16[4,1040,512]{2,1,0:T(8,128)(2,1)}, u32[]{:S(2)}, u32[]{:S(2)}) async-start(bf16[4,1040,512]{2,1,0:T(8,128)(2,1)} %get-tuple-element.20), calls=%async_computation | async-start | bytes 8519680 | tf_op jit(solution)/shard_map/all_to_all | solution.py:301
  27.1 0.7 collective-permute-start.4
  27.9 1.3 collective-permute-start.5
  29.2 1.3 collective-permute-start.6
  30.5 1.3 collective-permute-start.7
  31.8 6.0 %shard_map.28 = (f32[256,512]{1,0:T(8,128)}, bf16[256,512]{1,0:T(8,128)(2,1)}) custom-call(s32[2]{0:T(128)} %pad_add_fusion.place, bf16[4096,512]{1,0:T(8,128)(2,1)} %data.3, f32[3,512]{1,0:T(4,128)} %pad_maximum_fusion.1.stats), custom_call_target="tpu_custom_call" | custom-call | tf_op jit(solution)/shard_map/pallas_call | solution.py:142
  37.8 0.6 collective-permute-start.2
  38.5 1.3 collective-permute-done.2
  39.8 1.8 fusion.22.refs_0_
  41.6 78.7 %all-to-all-done.raw = bf16[4,1040,512]{2,1,0:T(8,128)(2,1)} async-done(((bf16[4,1040,512]{2,1,0:T(8,128)(2,1)}), bf16[4,1040,512]{2,1,0:T(8,128)(2,1)}, u32[]{:S(2)}, u32[]{:S(2)}) %all-to-all-start) | async-done | bytes 4259872 | tf_op jit(solution)/shard_map/all_to_all | solution.py:301
  120.4 6.7 %shard_map.30 = (bf16[8,1024,512]{2,1,0:T(8,128)(2,1)}, bf16[4,1024,256]{2,1,0:T(8,128)(2,1)}, bf16[4,1024,256]{2,1,0:T(8,128)(2,1)}, f32[4,3,512]{2,1,0:T(4,128)}) custom-call(s32[2]{0:T(128)} %pad_add_fusion.place, bf16[4,1040,512]{2,1,0:T(8,128)(2,1)} %all-to-all-done.raw, bf16[256,512]{1,0:T(8,128)(2,1)} %fusion.22.refs_0_), custom_call_target="tpu_custom_call" | custom-call | tf_op jit(solution)/shard_map/pallas_call | solution.py:179
  127.2 15.6 %collective-permute-done.7.refs_3_ = bf16[1040,512]{1,0:T(8,128)(2,1)} collective-permute-done((bf16[1040,512]{1,0:T(8,128)(2,1)}, bf16[1040,512]{1,0:T(8,128)(2,1)}, u32[]{:S(2)}, u32[]{:S(2)}) %collective-permute-start.7) | collective-permute-done | bytes 1064992 | tf_op jit(solution)/shard_map/ppermute | solution.py:15
  142.8 5.6 %shard_map.31 = (bf16[8,1024,512]{2,1,0:T(8,128)(2,1)}, f32[4,3,512]{2,1,0:T(4,128)}) custom-call(s32[2]{0:T(128)} %pad_add_fusion.place, bf16[1040,512]{1,0:T(8,128)(2,1)} %copy-done.4, bf16[1040,512]{1,0:T(8,128)(2,1)} %copy-done.5, bf16[1040,512]{1,0:T(8,128)(2,1)} %copy-done.6, ...), custom_call_target="tpu_custom_call", output_to_operand_aliasing={{0}: (5, {})} | custom-call | tf_op jit(solution)/shard_map/pallas_call | solution.py:208
  148.4 3.6 %fusion.13 = bf16[4,256,512]{2,1,0:T(8,128)(2,1)S(1)} fusion(bf16[4,1024,256]{2,1,0:T(8,128)(2,1)S(1)} %copy-done.16, bf16[8,1024,512]{2,1,0:T(8,128)(2,1)} %get-tuple-element.27), kind=kOutput, calls=%fused_computation.15 | convolution fusion | flops 1074266112 | bytes 7340032 | tf_op jit(solution)/shard_map/zsa,zsb->zab/dot_general | solution.py:329
  152.1 1.0 copy-done.2
  153.0 1.3 fusion.19
  154.4 1.3 fusion.16
  155.7 0.8 slice.46
  156.5 1.3 fusion.11
  157.8 1.6 collective-permute-start.8
  159.9 1.3 fusion.3
  161.2 1.3 fusion.7
  163.0 1.5 collective-permute-start.10
  164.6 6.0 %collective-permute-done.9.refs_0_ = bf16[256,512]{1,0:T(8,128)(2,1)S(1)} collective-permute-done((bf16[256,512]{1,0:T(8,128)(2,1)S(1)}, bf16[256,512]{1,0:T(8,128)(2,1)S(1)}, u32[]{:S(2)}, u32[]{:S(2)}) %collective-permute-start.9) | collective-permute-done | bytes 262176 | tf_op jit(solution)/shard_map/ppermute | solution.py:15
  170.6 5.6 %collective-permute-start.3 = (bf16[256,512]{1,0:T(8,128)(2,1)S(1)}, bf16[256,512]{1,0:T(8,128)(2,1)S(1)}, u32[]{:S(2)}, u32[]{:S(2)}) collective-permute-start(bf16[256,512]{1,0:T(8,128)(2,1)S(1)} %copy-done.3), channel_id=1, source_target_pairs={{0,2},{1,3},{2,0},{3,1},{4,6},{5,7},{6,4},{7,5},{8,10},{9,11},{10,... | collective-permute-start | bytes 786440 | tf_op jit(solution)/shard_map/ppermute | solution.py:15
  176.2 1.3 collective-permute-done.10.refs_1_
  177.6 5.7 %collective-permute-start.12 = (bf16[256,512]{1,0:T(8,128)(2,1)S(1)}, bf16[256,512]{1,0:T(8,128)(2,1)S(1)}, u32[]{:S(2)}, u32[]{:S(2)}) collective-permute-start(bf16[256,512]{1,0:T(8,128)(2,1)S(1)} %shard_map.32), channel_id=1, source_target_pairs={{0,2},{1,3},{2,0},{3,1},{4,6},{5,7},{6,4},{7,5},{8,10},{9,11},{10,... | collective-permute-start | bytes 786440 | tf_op jit(solution)/shard_map/ppermute | solution.py:15
  183.7 1.2 collective-permute-start.20
  185.2 1.3 collective-permute-start.22
  186.9 1.1 collective-permute-start.14
  188.1 2.2 collective-permute-done.12
  190.7 1.9 collective-permute-start.23
  192.6 6.8 %collective-permute-start.15 = (bf16[256,512]{1,0:T(8,128)(2,1)S(1)}, bf16[256,512]{1,0:T(8,128)(2,1)S(1)}, u32[]{:S(2)}, u32[]{:S(2)}) collective-permute-start(bf16[256,512]{1,0:T(8,128)(2,1)S(1)} %get-tuple-element.42), channel_id=1, source_target_pairs={{0,12},{1,13},{2,14},{3,15},{4,0},{5,1},{6,2},{7,3},{8,4},{9,5},{1... | collective-permute-start | bytes 786440 | tf_op jit(solution)/shard_map/ppermute | solution.py:15
  199.4 3.9 %collective-permute-start.16 = (bf16[256,512]{1,0:T(8,128)(2,1)S(1)}, bf16[256,512]{1,0:T(8,128)(2,1)S(1)}, u32[]{:S(2)}, u32[]{:S(2)}) collective-permute-start(bf16[256,512]{1,0:T(8,128)(2,1)S(1)} %get-tuple-element.41), channel_id=1, source_target_pairs={{0,8},{1,9},{2,10},{3,11},{4,12},{5,13},{6,14},{7,15},{8,0},{9,1},... | collective-permute-start | bytes 786440 | tf_op jit(solution)/shard_map/ppermute | solution.py:15
  204.1 5.1 %collective-permute-start.24 = (bf16[256,512]{1,0:T(8,128)(2,1)S(1)}, bf16[256,512]{1,0:T(8,128)(2,1)S(1)}, u32[]{:S(2)}, u32[]{:S(2)}) collective-permute-start(bf16[256,512]{1,0:T(8,128)(2,1)S(1)} %shard_map.34), channel_id=1, source_target_pairs={{0,2},{1,3},{2,0},{3,1},{4,6},{5,7},{6,4},{7,5},{8,10},{9,11},{10,... | collective-permute-start | bytes 786440 | tf_op jit(solution)/shard_map/ppermute | solution.py:15
  209.2 5.5 %collective-permute-done.16.refs_2_ = bf16[256,512]{1,0:T(8,128)(2,1)S(1)} collective-permute-done((bf16[256,512]{1,0:T(8,128)(2,1)S(1)}, bf16[256,512]{1,0:T(8,128)(2,1)S(1)}, u32[]{:S(2)}, u32[]{:S(2)}) %collective-permute-start.16) | collective-permute-done | bytes 262176 | tf_op jit(solution)/shard_map/ppermute | solution.py:15
  214.9 5.7 %collective-permute-start.18 = (bf16[256,512]{1,0:T(8,128)(2,1)S(1)}, bf16[256,512]{1,0:T(8,128)(2,1)S(1)}, u32[]{:S(2)}, u32[]{:S(2)}) collective-permute-start(bf16[256,512]{1,0:T(8,128)(2,1)S(1)} %shard_map.33), channel_id=1, source_target_pairs={{0,2},{1,3},{2,0},{3,1},{4,6},{5,7},{6,4},{7,5},{8,10},{9,11},{10,... | collective-permute-start | bytes 786440 | tf_op jit(solution)/shard_map/ppermute | solution.py:15
  220.6 16.4 %collective-permute-done.18 = bf16[256,512]{1,0:T(8,128)(2,1)S(1)} collective-permute-done((bf16[256,512]{1,0:T(8,128)(2,1)S(1)}, bf16[256,512]{1,0:T(8,128)(2,1)S(1)}, u32[]{:S(2)}, u32[]{:S(2)}) %collective-permute-start.18) | collective-permute-done | bytes 262176 | tf_op jit(solution)/shard_map/ppermute | solution.py:15
  237.3 0.8 collective-permute-start.25
  238.3 1.1 collective-permute-done.25.refs_6_
  240.0 0.7 copy-done.12
  240.7 3.0 %shard_map.35 = bf16[512,2048]{1,0:T(8,128)(2,1)} custom-call(s32[2]{0:T(128)} %pad_add_fusion.place, bf16[256,512]{1,0:T(8,128)(2,1)} %copy-done.8, bf16[256,512]{1,0:T(8,128)(2,1)} %copy-done.7, bf16[256,512]{1,0:T(8,128)(2,1)} %copy-done.10, bf16[256,512]{1,0:T(8,128)(2,1)} %copy-done.9, bf16[256,512]{1,0:T(8,128)(2,1)} %copy-done.1, ...), custom_call_target="tpu_custom_call" | custom-call | tf_op jit(solution)/shard_map/pallas_call | solution.py:267
  (79 shorter events, 5.7 us)
Async XLA Ops:
  3.3 8.0 %collective-permute-start = (f32[2,512]{1,0:T(2,128)S(1)}, f32[2,512]{1,0:T(2,128)S(1)}, u32[]{:S(2)}, u32[]{:S(2)}) collective-permute-start(f32[2,512]{1,0:T(2,128)S(1)} %get-tuple-element.53), channel_id=1, source_target_pairs={{0,2},{1,3},{2,0},{3,1},{4,6},{5,7},{6,4},{7,5},{8,10},{9,11},{10,... | collective-permute-start | bytes 12296 | tf_op jit(solution)/shard_map/ppermute | solution.py:15
  11.3 2.4 collective-permute-start.1
  22.1 98.3 %all-to-all-start = ((bf16[4,1040,512]{2,1,0:T(8,128)(2,1)}), bf16[4,1040,512]{2,1,0:T(8,128)(2,1)}, u32[]{:S(2)}, u32[]{:S(2)}) async-start(bf16[4,1040,512]{2,1,0:T(8,128)(2,1)} %get-tuple-element.20), calls=%async_computation | async-start | bytes 8519680 | tf_op jit(solution)/shard_map/all_to_all | solution.py:301
  27.1 100.0 %collective-permute-start.4 = (bf16[1040,512]{1,0:T(8,128)(2,1)}, bf16[1040,512]{1,0:T(8,128)(2,1)S(1)}, u32[]{:S(2)}, u32[]{:S(2)}) collective-permute-start(bf16[1040,512]{1,0:T(8,128)(2,1)} %get-tuple-element.22), channel_id=1, source_target_pairs={{16,0},{17,1},{18,2},{19,3},{20,4},{21,5},{22,6},{23,7},{24,8},{25... | collective-permute-start | bytes 3194888 | tf_op jit(solution)/shard_map/ppermute | solution.py:15
  27.9 99.3 %collective-permute-start.5 = (bf16[1040,512]{1,0:T(8,128)(2,1)}, bf16[1040,512]{1,0:T(8,128)(2,1)S(1)}, u32[]{:S(2)}, u32[]{:S(2)}) collective-permute-start(bf16[1040,512]{1,0:T(8,128)(2,1)} %get-tuple-element.23), channel_id=1, source_target_pairs={{16,12},{17,13},{18,14},{19,15},{20,0},{21,1},{22,2},{23,3},{24,4}... | collective-permute-start | bytes 3194888 | tf_op jit(solution)/shard_map/ppermute | solution.py:15
  29.2 98.0 %collective-permute-start.6 = (bf16[1040,512]{1,0:T(8,128)(2,1)}, bf16[1040,512]{1,0:T(8,128)(2,1)S(1)}, u32[]{:S(2)}, u32[]{:S(2)}) collective-permute-start(bf16[1040,512]{1,0:T(8,128)(2,1)} %get-tuple-element.24), channel_id=1, source_target_pairs={{16,8},{17,9},{18,10},{19,11},{20,12},{21,13},{22,14},{23,15},{24,... | collective-permute-start | bytes 3194888 | tf_op jit(solution)/shard_map/ppermute | solution.py:15
  30.5 8.0 %copy-start.14 = (s32[512]{0:T(512)S(1)}, s32[512]{0:T(512)}, u32[]{:S(2)}) copy-start(s32[512]{0:T(512)} %param.3) | copy-start | bytes 6148
  30.5 112.3 %collective-permute-start.7 = (bf16[1040,512]{1,0:T(8,128)(2,1)}, bf16[1040,512]{1,0:T(8,128)(2,1)}, u32[]{:S(2)}, u32[]{:S(2)}) collective-permute-start(bf16[1040,512]{1,0:T(8,128)(2,1)} %get-tuple-element.25), channel_id=1, source_target_pairs={{16,4},{17,5},{18,6},{19,7},{20,8},{21,9},{22,10},{23,11},{24,12},... | collective-permute-start | bytes 3194888 | tf_op jit(solution)/shard_map/ppermute | solution.py:15
  37.8 2.0 collective-permute-start.2
  127.1 15.6 %copy-start.4 = (bf16[1040,512]{1,0:T(8,128)(2,1)}, bf16[1040,512]{1,0:T(8,128)(2,1)S(1)}, u32[]{:S(2)}) copy-start(bf16[1040,512]{1,0:T(8,128)(2,1)S(1)} %collective-permute-done.4.refs_0_) | copy-start | bytes 3194884
  127.1 15.6 %copy-start.5 = (bf16[1040,512]{1,0:T(8,128)(2,1)}, bf16[1040,512]{1,0:T(8,128)(2,1)S(1)}, u32[]{:S(2)}) copy-start(bf16[1040,512]{1,0:T(8,128)(2,1)S(1)} %collective-permute-done.5.refs_1_) | copy-start | bytes 3194884
  127.2 15.6 %copy-start.6 = (bf16[1040,512]{1,0:T(8,128)(2,1)}, bf16[1040,512]{1,0:T(8,128)(2,1)S(1)}, u32[]{:S(2)}) copy-start(bf16[1040,512]{1,0:T(8,128)(2,1)S(1)} %collective-permute-done.6.refs_2_) | copy-start | bytes 3194884
  142.8 5.6 %copy-start.16 = (bf16[4,1024,256]{2,1,0:T(8,128)(2,1)S(1)}, bf16[4,1024,256]{2,1,0:T(8,128)(2,1)}, u32[]{:S(2)}) copy-start(bf16[4,1024,256]{2,1,0:T(8,128)(2,1)} %get-tuple-element.28) | copy-start | bytes 6291460
  148.4 4.6 %copy-start.2 = (bf16[8,1024,512]{2,1,0:T(8,128)(2,1)S(1)}, bf16[8,1024,512]{2,1,0:T(8,128)(2,1)}, u32[]{:S(2)}) copy-start(bf16[8,1024,512]{2,1,0:T(8,128)(2,1)} %get-tuple-element.27) | copy-start | bytes 25165828
  154.3 1.3 copy-start.13
  154.4 2.1 copy-start.15
  157.8 4.7 %collective-permute-start.8 = (bf16[4,256,512]{2,1,0:T(8,128)(2,1)S(1)}, bf16[4,256,512]{2,1,0:T(8,128)(2,1)S(1)}, u32[]{:S(2)}, u32[]{:S(2)}) collective-permute-start(bf16[4,256,512]{2,1,0:T(8,128)(2,1)S(1)} %fusion.13), channel_id=1, source_target_pairs={{0,1},{1,0},{2,3},{3,2},{4,5},{5,4},{6,7},{7,6},{8,9},{9,8},{10,11... | collective-permute-start | bytes 3145736 | tf_op jit(solution)/shard_map/ppermute | solution.py:15
  159.4 24.0 %collective-permute-start.19 = (bf16[4,256,512]{2,1,0:T(8,128)(2,1)S(1)}, bf16[4,256,512]{2,1,0:T(8,128)(2,1)S(1)}, u32[]{:S(2)}, u32[]{:S(2)}) collective-permute-start(bf16[4,256,512]{2,1,0:T(8,128)(2,1)S(1)} %fusion.19), channel_id=1, source_target_pairs={{0,1},{1,0},{2,3},{3,2},{4,5},{5,4},{6,7},{7,6},{8,9},{9,8},{10,11... | collective-permute-start | bytes 3145736 | tf_op jit(solution)/shard_map/ppermute | solution.py:15
  159.6 25.6 %collective-permute-start.13 = (bf16[4,256,512]{2,1,0:T(8,128)(2,1)S(1)}, bf16[4,256,512]{2,1,0:T(8,128)(2,1)S(1)}, u32[]{:S(2)}, u32[]{:S(2)}) collective-permute-start(bf16[4,256,512]{2,1,0:T(8,128)(2,1)S(1)} %fusion.16), channel_id=1, source_target_pairs={{0,1},{1,0},{2,3},{3,2},{4,5},{5,4},{6,7},{7,6},{8,9},{9,8},{10,11... | collective-permute-start | bytes 3145736 | tf_op jit(solution)/shard_map/ppermute | solution.py:15
  162.5 8.1 %copy-start.3 = (bf16[256,512]{1,0:T(8,128)(2,1)S(1)}, bf16[256,512]{1,0:T(8,128)(2,1)}, u32[]{:S(2)}) copy-start(bf16[256,512]{1,0:T(8,128)(2,1)} %fusion.22.refs_0_) | copy-start | bytes 786436
  162.9 7.7 %collective-permute-start.9 = (bf16[256,512]{1,0:T(8,128)(2,1)S(1)}, bf16[256,512]{1,0:T(8,128)(2,1)S(1)}, u32[]{:S(2)}, u32[]{:S(2)}) collective-permute-start(bf16[256,512]{1,0:T(8,128)(2,1)S(1)} %get-tuple-element.47), channel_id=1, source_target_pairs={{0,4},{1,5},{2,6},{3,7},{4,8},{5,9},{6,10},{7,11},{8,12},{9,13},{1... | collective-permute-start | bytes 786440 | tf_op jit(solution)/shard_map/ppermute | solution.py:15
  163.0 14.5 %collective-permute-start.10 = (bf16[256,512]{1,0:T(8,128)(2,1)S(1)}, bf16[256,512]{1,0:T(8,128)(2,1)S(1)}, u32[]{:S(2)}, u32[]{:S(2)}) collective-permute-start(bf16[256,512]{1,0:T(8,128)(2,1)S(1)} %get-tuple-element.46), channel_id=1, source_target_pairs={{0,12},{1,13},{2,14},{3,15},{4,0},{5,1},{6,2},{7,3},{8,4},{9,5},{1... | collective-permute-start | bytes 786440 | tf_op jit(solution)/shard_map/ppermute | solution.py:15
  164.4 13.1 %collective-permute-start.11 = (bf16[256,512]{1,0:T(8,128)(2,1)S(1)}, bf16[256,512]{1,0:T(8,128)(2,1)S(1)}, u32[]{:S(2)}, u32[]{:S(2)}) collective-permute-start(bf16[256,512]{1,0:T(8,128)(2,1)S(1)} %get-tuple-element.45), channel_id=1, source_target_pairs={{0,8},{1,9},{2,10},{3,11},{4,12},{5,13},{6,14},{7,15},{8,0},{9,1},... | collective-permute-start | bytes 786440 | tf_op jit(solution)/shard_map/ppermute | solution.py:15
  170.6 16.4 %collective-permute-start.3 = (bf16[256,512]{1,0:T(8,128)(2,1)S(1)}, bf16[256,512]{1,0:T(8,128)(2,1)S(1)}, u32[]{:S(2)}, u32[]{:S(2)}) collective-permute-start(bf16[256,512]{1,0:T(8,128)(2,1)S(1)} %copy-done.3), channel_id=1, source_target_pairs={{0,2},{1,3},{2,0},{3,1},{4,6},{5,7},{6,4},{7,5},{8,10},{9,11},{10,... | collective-permute-start | bytes 786440 | tf_op jit(solution)/shard_map/ppermute | solution.py:15
  177.6 12.7 %collective-permute-start.12 = (bf16[256,512]{1,0:T(8,128)(2,1)S(1)}, bf16[256,512]{1,0:T(8,128)(2,1)S(1)}, u32[]{:S(2)}, u32[]{:S(2)}) collective-permute-start(bf16[256,512]{1,0:T(8,128)(2,1)S(1)} %shard_map.32), channel_id=1, source_target_pairs={{0,2},{1,3},{2,0},{3,1},{4,6},{5,7},{6,4},{7,5},{8,10},{9,11},{10,... | collective-permute-start | bytes 786440 | tf_op jit(solution)/shard_map/ppermute | solution.py:15
  183.7 8.9 %collective-permute-start.20 = (bf16[256,512]{1,0:T(8,128)(2,1)S(1)}, bf16[256,512]{1,0:T(8,128)(2,1)S(1)}, u32[]{:S(2)}, u32[]{:S(2)}) collective-permute-start(bf16[256,512]{1,0:T(8,128)(2,1)S(1)} %get-tuple-element.39), channel_id=1, source_target_pairs={{0,4},{1,5},{2,6},{3,7},{4,8},{5,9},{6,10},{7,11},{8,12},{9,13},{1... | collective-permute-start | bytes 786440 | tf_op jit(solution)/shard_map/ppermute | solution.py:15
  184.9 14.5 %collective-permute-start.21 = (bf16[256,512]{1,0:T(8,128)(2,1)S(1)}, bf16[256,512]{1,0:T(8,128)(2,1)S(1)}, u32[]{:S(2)}, u32[]{:S(2)}) collective-permute-start(bf16[256,512]{1,0:T(8,128)(2,1)S(1)} %get-tuple-element.38), channel_id=1, source_target_pairs={{0,12},{1,13},{2,14},{3,15},{4,0},{5,1},{6,2},{7,3},{8,4},{9,5},{1... | collective-permute-start | bytes 786440 | tf_op jit(solution)/shard_map/ppermute | solution.py:15
  185.2 18.1 %collective-permute-start.22 = (bf16[256,512]{1,0:T(8,128)(2,1)S(1)}, bf16[256,512]{1,0:T(8,128)(2,1)S(1)}, u32[]{:S(2)}, u32[]{:S(2)}) collective-permute-start(bf16[256,512]{1,0:T(8,128)(2,1)S(1)} %get-tuple-element.37), channel_id=1, source_target_pairs={{0,8},{1,9},{2,10},{3,11},{4,12},{5,13},{6,14},{7,15},{8,0},{9,1},... | collective-permute-start | bytes 786440 | tf_op jit(solution)/shard_map/ppermute | solution.py:15
  186.9 22.3 %collective-permute-start.14 = (bf16[256,512]{1,0:T(8,128)(2,1)S(1)}, bf16[256,512]{1,0:T(8,128)(2,1)S(1)}, u32[]{:S(2)}, u32[]{:S(2)}) collective-permute-start(bf16[256,512]{1,0:T(8,128)(2,1)S(1)} %get-tuple-element.43), channel_id=1, source_target_pairs={{0,4},{1,5},{2,6},{3,7},{4,8},{5,9},{6,10},{7,11},{8,12},{9,13},{1... | collective-permute-start | bytes 786440 | tf_op jit(solution)/shard_map/ppermute | solution.py:15
  190.7 24.1 %copy-start.7 = (bf16[256,512]{1,0:T(8,128)(2,1)}, bf16[256,512]{1,0:T(8,128)(2,1)S(1)}, u32[]{:S(2)}) copy-start(bf16[256,512]{1,0:T(8,128)(2,1)S(1)} %get-tuple-element.57.refs_1_) | copy-start | bytes 786436
  190.7 24.1 %copy-start.8 = (bf16[256,512]{1,0:T(8,128)(2,1)}, bf16[256,512]{1,0:T(8,128)(2,1)S(1)}, u32[]{:S(2)}) copy-start(bf16[256,512]{1,0:T(8,128)(2,1)S(1)} %get-tuple-element.59.refs_0_) | copy-start | bytes 786436
  190.7 13.2 %collective-permute-start.23 = (bf16[256,512]{1,0:T(8,128)(2,1)S(1)}, bf16[256,512]{1,0:T(8,128)(2,1)S(1)}, u32[]{:S(2)}, u32[]{:S(2)}) collective-permute-start(bf16[256,512]{1,0:T(8,128)(2,1)S(1)} %get-tuple-element.57.refs_1_), channel_id=1, source_target_pairs={{0,1},{1,0},{2,3},{3,2},{4,5},{5,4},{6,7},{7,6},{8,9},{9,8},{10,11... | collective-permute-start | bytes 786440 | tf_op jit(solution)/shard_map/ppermute | solution.py:15
  192.6 16.6 %collective-permute-start.15 = (bf16[256,512]{1,0:T(8,128)(2,1)S(1)}, bf16[256,512]{1,0:T(8,128)(2,1)S(1)}, u32[]{:S(2)}, u32[]{:S(2)}) collective-permute-start(bf16[256,512]{1,0:T(8,128)(2,1)S(1)} %get-tuple-element.42), channel_id=1, source_target_pairs={{0,12},{1,13},{2,14},{3,15},{4,0},{5,1},{6,2},{7,3},{8,4},{9,5},{1... | collective-permute-start | bytes 786440 | tf_op jit(solution)/shard_map/ppermute | solution.py:15
  199.4 15.3 %collective-permute-start.16 = (bf16[256,512]{1,0:T(8,128)(2,1)S(1)}, bf16[256,512]{1,0:T(8,128)(2,1)S(1)}, u32[]{:S(2)}, u32[]{:S(2)}) collective-permute-start(bf16[256,512]{1,0:T(8,128)(2,1)S(1)} %get-tuple-element.41), channel_id=1, source_target_pairs={{0,8},{1,9},{2,10},{3,11},{4,12},{5,13},{6,14},{7,15},{8,0},{9,1},... | collective-permute-start | bytes 786440 | tf_op jit(solution)/shard_map/ppermute | solution.py:15
  203.3 11.4 %collective-permute-start.17 = (bf16[256,512]{1,0:T(8,128)(2,1)S(1)}, bf16[256,512]{1,0:T(8,128)(2,1)S(1)}, u32[]{:S(2)}, u32[]{:S(2)}) collective-permute-start(bf16[256,512]{1,0:T(8,128)(2,1)S(1)} %get-tuple-element.59.refs_0_), channel_id=1, source_target_pairs={{0,1},{1,0},{2,3},{3,2},{4,5},{5,4},{6,7},{7,6},{8,9},{9,8},{10,11... | collective-permute-start | bytes 786440 | tf_op jit(solution)/shard_map/ppermute | solution.py:15
  203.9 10.9 %copy-start = (bf16[256,512]{1,0:T(8,128)(2,1)}, bf16[256,512]{1,0:T(8,128)(2,1)S(1)}, u32[]{:S(2)}) copy-start(bf16[256,512]{1,0:T(8,128)(2,1)S(1)} %collective-permute-done.23.refs_4_.refs_5_) | copy-start | bytes 786436
  204.1 16.5 %collective-permute-start.24 = (bf16[256,512]{1,0:T(8,128)(2,1)S(1)}, bf16[256,512]{1,0:T(8,128)(2,1)S(1)}, u32[]{:S(2)}, u32[]{:S(2)}) collective-permute-start(bf16[256,512]{1,0:T(8,128)(2,1)S(1)} %shard_map.34), channel_id=1, source_target_pairs={{0,2},{1,3},{2,0},{3,1},{4,6},{5,7},{6,4},{7,5},{8,10},{9,11},{10,... | collective-permute-start | bytes 786440 | tf_op jit(solution)/shard_map/ppermute | solution.py:15
  214.7 25.0 %copy-start.1 = (bf16[256,512]{1,0:T(8,128)(2,1)}, bf16[256,512]{1,0:T(8,128)(2,1)S(1)}, u32[]{:S(2)}) copy-start(bf16[256,512]{1,0:T(8,128)(2,1)S(1)} %collective-permute-done.17.refs_4_) | copy-start | bytes 786436
  214.9 22.1 %collective-permute-start.18 = (bf16[256,512]{1,0:T(8,128)(2,1)S(1)}, bf16[256,512]{1,0:T(8,128)(2,1)S(1)}, u32[]{:S(2)}, u32[]{:S(2)}) collective-permute-start(bf16[256,512]{1,0:T(8,128)(2,1)S(1)} %shard_map.33), channel_id=1, source_target_pairs={{0,2},{1,3},{2,0},{3,1},{4,6},{5,7},{6,4},{7,5},{8,10},{9,11},{10,... | collective-permute-start | bytes 786440 | tf_op jit(solution)/shard_map/ppermute | solution.py:15
  237.3 2.4 copy-start.9
  237.3 2.4 copy-start.10
  237.3 2.0 collective-permute-start.25
  238.2 1.5 collective-permute-start.26
  239.3 0.7 copy-start.11
  240.0 0.7 copy-start.12
